TPU v7x, 32 devices: a whole 2x2x4 slice. The times are simulated.
32 devices in a mesh: parts: 2 (over x), rows: 16 (over z, y, core).
Axes of the slice: x: 2, y: 2, z: 4, core: 2. Of those that a mesh axis runs over, the one named last changes fastest.
Arguments:
- traces: bfloat16 [16, 4096, 2048], P('parts', 'rows'), parts along dimension 0, may hold values from -6 to 6
- offset_bin: int32 [16, 4096], P('parts', 'rows'), parts along dimension 0, may hold values from 0 to 15
- filters: float32 [16, 32], replicated, may hold values from -1 to 1
- data_matrix: bfloat16 [128, 2, 64, 4096], P('parts', None, 'rows'), parts along dimension 0, may hold values from -0.0625 to 0.0625
Outputs:
- multiples: bfloat16 [128, 2, 8, 64], P(('parts', 'rows')), parts along dimension 0
There are 2 independent parts, one for each index of `parts`. A program takes and returns all parts, laid end to end along the dimension named above; an argument that names none is the same for every part. Nothing has to cross between parts.
All inputs are finite; a program needn't handle non-finite values.
Results may differ from a plain program's by a relative error of at most 0.0067.
Values may be sent and summed in bfloat16 or wider, within the bound.
A program may use at most 128 MiB of HBM per device.

v0:
```python
import math

import jax
import jax.numpy as jnp
from jax import lax
from jax.sharding import PartitionSpec as P

FIRST = 64


def spectral_table(freq_count, first_index, length):
    freq_index = first_index + jnp.arange(freq_count, dtype=jnp.int32)
    sample_index = jnp.arange(length, dtype=jnp.int32)
    product_index = freq_index[:, None] * sample_index[None, :] % length
    phase_angle = product_index.astype(jnp.float32) * jnp.float32(2.0 * math.pi / length)
    norm_factor = jnp.float32(1.0 / math.sqrt(length))
    stacked = jnp.stack([jnp.cos(phase_angle), -jnp.sin(phase_angle)], axis=1) * norm_factor
    return stacked.astype(jnp.bfloat16)


def condition(traces, offset_bin, filters):
    bin_count, tap_count = filters.shape
    length = traces.shape[2]
    selector = (
        offset_bin[:, :, None] == jnp.arange(bin_count, dtype=jnp.int32)[None, None, :]
    ).astype(jnp.float32)
    tap_rows = jnp.einsum("skb,bj->skj", selector, filters, precision=lax.Precision.HIGHEST)
    padded = jnp.pad(traces, ((0, 0), (0, 0), (tap_count - 1, 0)))
    filtered = jnp.zeros(traces.shape, jnp.float32)
    for delay_index in range(tap_count):
        window = padded[:, :, tap_count - 1 - delay_index : tap_count - 1 - delay_index + length]
        filtered = filtered + tap_rows[:, :, delay_index : delay_index + 1] * window.astype(
            jnp.float32
        )
    return filtered.astype(jnp.bfloat16)


def spectra_of(filtered, table):
    shot_count, receivers, length = filtered.shape
    flat_table = table.reshape(-1, length)
    flat_signal = filtered.reshape(shot_count * receivers, length)
    values = lax.dot_general(
        flat_table, flat_signal, (((1,), (1,)), ((), ())), preferred_element_type=jnp.float32
    )
    return values.astype(jnp.bfloat16).reshape(table.shape[0], 2, shot_count * receivers)


def predict(matrix_block, spectral_block):
    real_part = jnp.einsum(
        "tion,toun->tui",
        matrix_block[:, 0],
        spectral_block[:, 0],
        preferred_element_type=jnp.float32,
    ) - jnp.einsum(
        "tion,toun->tui",
        matrix_block[:, 1],
        spectral_block[:, 1],
        preferred_element_type=jnp.float32,
    )
    imag_part = jnp.einsum(
        "tion,toun->tui",
        matrix_block[:, 0],
        spectral_block[:, 1],
        preferred_element_type=jnp.float32,
    ) + jnp.einsum(
        "tion,toun->tui",
        matrix_block[:, 1],
        spectral_block[:, 0],
        preferred_element_type=jnp.float32,
    )
    return jnp.stack([real_part, imag_part], axis=1)


def shards(traces, offset_bin, filters, data_matrix):
    shot_count, receivers, length = traces.shape
    freq_count = data_matrix.shape[0]
    row_count = data_matrix.shape[2]
    table = spectral_table(freq_count, FIRST, length)
    spectra = spectra_of(condition(traces, offset_bin, filters), table)
    tile_width = shot_count * receivers
    gathered = lax.all_gather(spectra, "rows", axis=2, tiled=True)
    groups = gathered.shape[2] // tile_width
    matrix_block = data_matrix.reshape(freq_count, 2, row_count, groups, receivers)
    spectral_block = gathered.reshape(freq_count, 2, groups, shot_count, receivers)
    partial_value = predict(matrix_block, spectral_block)
    return lax.all_to_all(
        partial_value.astype(jnp.bfloat16), "rows", split_axis=0, concat_axis=3, tiled=True
    )


def solution(mesh):
    in_specs = (P("parts", "rows", None), P("parts", "rows"), P(), P("parts", None, "rows", None))
    out_specs = P(("parts", "rows"), None, None, None)
    return jax.shard_map(shards, mesh=mesh, in_specs=in_specs, out_specs=out_specs, check_vma=False)
```

profile of v0, /device:TPU:0, one launch (start us, length us, event | category | flops | bytes accessed | tf_op | source)
XLA Modules:
  0.0 367.7 jit_solution(11606199843413295791)
XLA Ops:
  6.5 0.7 copy-done
  7.2 1.0 fusion.22
  8.2 0.1 fusion.26
  8.4 0.1 fusion.27
  8.4 2.1 fusion.21
  10.6 0.1 fusion.14
  10.7 0.5 copy.36
  11.2 0.2 convert_element_type.137
  11.6 223.1 %add_convert_fusion = bf16[8,256,2048]{2,1,0:T(8,128)(2,1)} fusion(bf16[8,256,2048]{2,1,0:T(8,128)(2,1)} %param.4, f32[8,256]{1,0:T(8,128)S(1)} %get-tuple-element.41, f32[8,256]{1,0:T(8,128)S(1)} %get-tuple-element.42, f32[8,256]{1,0:T(8,128)S(1)} %get-tuple-element.43, f32[8,256]{1,0:T(8,128)S(1)} %get-tuple-element.44, f32[8,256]{1,0:T(8,128)S(1)} %get-tuple-element.45, ...), kind=kLoop, calls=%fused_computation | loop fusion | flops 402653184 | bytes 17039360 | tf_op jit(solution)/shard_map/convert_element_type | solution.py:35
  234.8 6.3 %convolution_convert_fusion = bf16[128,2048]{1,0:T(8,128)(2,1)S(1)} fusion(bf16[128,2048]{1,0:T(8,128)(2,1)S(1)} %convert_element_type.137, bf16[2048,2048]{1,0:T(8,128)(2,1)} %bitcast.165), kind=kOutput, calls=%fused_computation.12 | convolution fusion | flops 1074003968 | bytes 9437184 | tf_op jit(solution)/shard_map/dot_general | solution.py:42
  241.0 1.2 reshape.123
  242.3 7.8 %reshape.132 = bf16[64,2,4,16,256]{4,3,2,1,0:T(8,128)(2,1)} reshape(bf16[64,2,4,4096]{3,2,1,0:T(4,128)(2,1)} %param.7) | data formatting | bytes 8388608 | tf_op jit(solution)/shard_map/reshape | solution.py:83
  250.1 4.1 %fusion.25 = (bf16[64,1,4,16,256]{4,3,2,1,0:T(8,128)(2,1)S(1)}, bf16[64,1,4,16,256]{4,3,2,1,0:T(8,128)(2,1)}) fusion(bf16[64,2,4,16,256]{4,3,2,1,0:T(8,128)(2,1)} %reshape.132), kind=kLoop, calls=%fused_computation.76 | loop fusion | bytes 8388608 | tf_op jit(solution)/shard_map/slice | solution.py:56
  254.1 69.1 %all-gather.2.cloned.1.call-done = bf16[64,2,32768]{2,1,0:T(2,128)(2,1)} async-done(((bf16[64,2,2048]{2,1,0:T(2,128)(2,1)}), bf16[64,2,32768]{2,1,0:T(2,128)(2,1)}) %all-gather.2.cloned.1.call-update) | async-done | bytes 8388624 | tf_op jit(solution)/shard_map/all_gather | solution.py:81
  323.2 14.1 %reshape.131 = bf16[64,2,16,8,256]{4,3,2,1,0:T(8,128)(2,1)} reshape(bf16[64,2,32768]{2,1,0:T(2,128)(2,1)} %all-gather.2.cloned.1.call-done) | data formatting | bytes 16777216 | tf_op jit(solution)/shard_map/reshape | solution.py:84
  337.3 5.3 %fusion.4 = f32[64,8,4]{1,2,0:T(4,128)S(1)} fusion(bf16[64,1,4,16,256]{4,3,2,1,0:T(8,128)(2,1)S(1)} %get-tuple-element.5, bf16[64,2,16,8,256]{4,3,2,1,0:T(8,128)(2,1)} %reshape.131), kind=kOutput, calls=%fused_computation.15 | convolution fusion | flops 16777216 | bytes 6299648 | tf_op jit(solution)/shard_map/tion,toun->tui/dot_general | solution.py:54
  342.7 3.0 fusion.5
  345.7 3.0 fusion.13
  348.7 1.7 fusion.12
  350.3 0.1 copy_bitcast_fusion.58
  350.4 0.2 reshape.133
  350.6 9.3 %all_to_all.18 = bf16[16,2,128]{2,1,0:T(2,128)(2,1)S(1)} all-to-all(bf16[16,2,128]{2,1,0:T(2,128)(2,1)S(1)} %reshape.133), channel_id=1, replica_groups=mesh['parts'=2,'rows'=16] {'rows'}, dimensions={0} | all-to-all | bytes 16384 | tf_op jit(solution)/shard_map/all_to_all | solution.py:86
  359.9 0.2 reshape.134
  360.2 0.7 copy.43
  (25 shorter events, 0.1 us)
Async XLA Ops:
  6.5 0.7 copy-start
  6.5 316.7 %all-gather.2.cloned.1.call-start = ((), (), s32[]{:S(2)}) async-start(), calls=%async_computation.1 | async-start | bytes 8912896 | tf_op jit(solution)/shard_map/all_gather | solution.py:81
  337.3 5.3 %copy-start.1 = (bf16[64,2,16,8,256]{4,3,2,1,0:T(8,128)(2,1)S(1)}, bf16[64,2,16,8,256]{4,3,2,1,0:T(8,128)(2,1)}, u32[]{:S(2)}) copy-start(bf16[64,2,16,8,256]{4,3,2,1,0:T(8,128)(2,1)} %reshape.131) | copy-start | bytes 25165828
  337.3 5.3 %copy-start.2 = (bf16[64,1,4,16,256]{4,3,2,1,0:T(8,128)(2,1)S(1)}, bf16[64,1,4,16,256]{4,3,2,1,0:T(8,128)(2,1)}, u32[]{:S(2)}) copy-start(bf16[64,1,4,16,256]{4,3,2,1,0:T(8,128)(2,1)} %get-tuple-element.6) | copy-start | bytes 6291460
Sparse Core Ops, SparseCore 0:
  242.4 80.7 all-gather.1
where the time goes:
time: 368 us
  other arithmetic  225 us (61%)
  waiting for transfers between devices  69.1 us (19%)
  local copies, waits for them, and re-layouts  30 us (8%)
  matrix products  20.2 us (5%)
  between operations  13.6 us (4%)
  blocking collectives  9.34 us (3%)
    convert_element_type x1, other arithmetic, condition(): return filtered.astype(jnp.bfloat16)  223 us
    all_gather x1, waiting for transfers between devices, shards(): gathered = lax.all_gather(spectra, 'rows', axis=2, tiled=True)  69.1 us
    reshape x1, local copies, waits for them, and re-layouts, shards(): gathered.reshape(freq_count, 2, groups, shot_count, receivers)  14.1 us
    all_to_all x1, blocking collectives, shards(): lax.all_to_all(partial_value.astype(jnp.bfloat16), 'rows', split_axis=0,...  9.34 us
    reshape x1, local copies, waits for them, and re-layouts, shards(): data_matrix.reshape(freq_count, 2, row_count, groups, receivers)  7.8 us
  transfers between devices with their start and end apart: 1, of which 1 were waited for; matrix products, arithmetic and copies ran while one was open for 3% of the time, Pallas kernels for 0%

commit v1 on v0

--- a/solution.py
+++ b/solution.py
@@ -1,11 +1,18 @@
+import functools
 import math
 
 import jax
 import jax.numpy as jnp
+import ml_dtypes
+import numpy as np
 from jax import lax
+from jax.experimental import pallas as pl
+from jax.experimental.pallas import tpu as pltpu
 from jax.sharding import PartitionSpec as P
 
 FIRST = 64
+GROUP = 16
+MESH = pl.DeviceIdType.MESH
 
 
 def spectral_table(freq_count, first_index, length):
@@ -71,7 +78,7 @@
     return jnp.stack([real_part, imag_part], axis=1)
 
 
-def shards(traces, offset_bin, filters, data_matrix):
+def plain(traces, offset_bin, filters, data_matrix):
     shot_count, receivers, length = traces.shape
     freq_count = data_matrix.shape[0]
     row_count = data_matrix.shape[2]
@@ -88,7 +95,297 @@
     )
 
 
+def phases(index, length):
+    angle = (index % length).astype(np.float64) * (2.0 * math.pi / length)
+    return np.cos(angle), -np.sin(angle)
+
+
+def constants(freq_count, length, taps, bins):
+    freq = FIRST + np.arange(freq_count, dtype=np.int64)
+    norm = 1.0 / math.sqrt(length)
+    head = np.stack(phases(freq[:, None] * np.arange(length)[None], length)) * norm
+    head[:, :, length - taps :] = 0.0
+    head = head.reshape(2 * freq_count, length).astype(np.float32).astype(ml_dtypes.bfloat16)
+    lag = np.stack(phases(freq[:, None] * np.arange(taps)[None], length))
+    lag = lag.reshape(2 * freq_count, taps).astype(np.float32)
+    last = np.stack(phases(freq[:, None] * (length - taps + np.arange(taps))[None], length)) * norm
+    last = np.tile(last, (1, 1, bins)).astype(np.float32)
+    return head, lag, last
+
+
+def fused_kernel(
+    dims, traces_hbm, bins_ref, filters_ref, cut_ref, head_ref, lag_ref, last_ref, matrix_hbm,
+    out_ref,
+    traces_buf, spectra, matrix_buf, total, tail_ref, folded, partials, landed,
+    trace_sem, own_sem, pair_send, pair_recv,
+    right_send, right_recv, left_send, left_recv, out_send, out_recv,
+):
+    n, shots, receivers, length, freqs, taps, bin_count, rows = dims
+    chips, half = n // 2, n // 4
+    groups = freqs // GROUP
+    width = GROUP * 2 * rows
+    me = lax.axis_index("rows")
+    chip, core = me // 2, me % 2
+    place = jnp.where(chip % 2 == 0, chip // 2, chips - 1 - chip // 2)
+
+    def chip_at(position):
+        position = (position + 2 * chips) % chips
+        return jnp.where(position < half, 2 * position, 2 * (chips - 1 - position) + 1)
+
+    right = chip_at(place + 1) * 2 + core
+    left = chip_at(place - 1) * 2 + core
+    sibling = chip * 2 + 1 - core
+
+    def trace_copy(shot):
+        return pltpu.make_async_copy(traces_hbm.at[shot], traces_buf.at[shot], trace_sem.at[shot])
+
+    for shot in range(shots):
+        trace_copy(shot).start()
+
+    barrier = pltpu.get_barrier_semaphore()
+    for step in range(1, n):
+        pl.semaphore_signal(
+            barrier, inc=1, device_id={"rows": (me + step) % n}, device_id_type=MESH
+        )
+
+    def columns(block, side):
+        return pl.ds(pl.multiple_of((block * 2 + side) * receivers, receivers), receivers)
+
+    def lanes():
+        return pl.ds(pl.multiple_of(core * width, width), width)
+
+    def own_copy(block):
+        return pltpu.make_async_copy(
+            matrix_hbm.at[:, :, columns(block, core)],
+            matrix_buf.at[block, :, lanes(), :],
+            own_sem.at[block],
+        )
+
+    def pair_copy(block):
+        return pltpu.make_async_remote_copy(
+            src_ref=matrix_hbm.at[:, :, columns(block, 1 - core)],
+            dst_ref=matrix_buf.at[block, :, lanes(), :],
+            send_sem=pair_send.at[block],
+            recv_sem=pair_recv.at[block],
+            device_id={"rows": sibling},
+            device_id_type=MESH,
+        )
+
+    def ring_copy(step, shot, rightward):
+        block = chip_at(place - (step - 1)) if rightward else chip_at(place + (step - 1))
+        send, recv = (right_send, right_recv) if rightward else (left_send, left_recv)
+        return pltpu.make_async_remote_copy(
+            src_ref=spectra.at[block, shot],
+            dst_ref=spectra.at[block, shot],
+            send_sem=send.at[step - 1, shot],
+            recv_sem=recv.at[step - 1, shot],
+            device_id={"rows": right if rightward else left},
+            device_id_type=MESH,
+        )
+
+    def arrival(step, shot, rightward):
+        block = chip_at(place - step) if rightward else chip_at(place + step)
+        send, recv = (right_send, right_recv) if rightward else (left_send, left_recv)
+        return pltpu.make_async_remote_copy(
+            src_ref=spectra.at[block, shot],
+            dst_ref=spectra.at[block, shot],
+            send_sem=send.at[step - 1, shot],
+            recv_sem=recv.at[step - 1, shot],
+            device_id={"rows": right if rightward else left},
+            device_id_type=MESH,
+        )
+
+    def reach(shot, rightward):
+        return half if (shot % 2 == 0) == rightward else half - 1
+
+    highest = lax.Precision.HIGHEST
+    contract = (((1,), (1,)), ((), ()))
+    gains = lax.dot_general(
+        lag_ref[...], filters_ref[...], contract, precision=highest,
+        preferred_element_type=jnp.float32,
+    )
+    cut = lax.dot_general(
+        lag_ref[...], cut_ref[...], contract, precision=highest,
+        preferred_element_type=jnp.float32,
+    )
+    cut_re, cut_im = cut[:freqs], cut[freqs:]
+    last_re, last_im = last_ref[0], last_ref[1]
+    tail_ref[:freqs] = (cut_re * last_re - cut_im * last_im).astype(jnp.bfloat16)
+    tail_ref[freqs:] = (cut_re * last_im + cut_im * last_re).astype(jnp.bfloat16)
+    bin_index = lax.broadcasted_iota(jnp.int32, (bin_count, receivers), 0)
+
+    for shot in range(shots):
+        trace_copy(shot).wait()
+        chosen = bins_ref[shot : shot + 1, :]
+        transform = lax.dot_general(
+            head_ref[...], traces_buf[shot], contract, preferred_element_type=jnp.float32
+        )
+        onehot = (bin_index == chosen).astype(jnp.float32)
+        gain = lax.dot_general(
+            gains, onehot, (((1,), (0,)), ((), ())), precision=highest,
+            preferred_element_type=jnp.float32,
+        )
+        ending = traces_buf[shot, :, length - 128 :].astype(jnp.float32).T[128 - taps :]
+        masked = jnp.concatenate(
+            [jnp.where(chosen == b, ending, 0.0) for b in range(bin_count)], axis=0
+        ).astype(jnp.bfloat16)
+        tail = jnp.dot(tail_ref[...], masked, preferred_element_type=jnp.float32)
+        re, im = transform[:freqs], transform[freqs:]
+        gain_re, gain_im = gain[:freqs], gain[freqs:]
+        spectra[chip, shot, 0] = (re * gain_re - im * gain_im + tail[:freqs]).astype(jnp.bfloat16)
+        spectra[chip, shot, 1] = (re * gain_im + im * gain_re + tail[freqs:]).astype(jnp.bfloat16)
+        if shot == 0:
+            pl.semaphore_wait(barrier, n - 1)
+        for rightward in (True, False):
+            ring_copy(1, shot, rightward).start()
+        if shot == 0:
+            for block in range(chips):
+                own_copy(block).start()
+                pair_copy(block).start()
+
+    def multiply(block, first=False):
+        for group in range(groups):
+            signal = spectra[block, :, :, group * GROUP : (group + 1) * GROUP, :]
+            product = lax.dot_general(
+                signal.reshape(shots * 2 * GROUP, receivers), matrix_buf[block, group], contract,
+                preferred_element_type=jnp.float32,
+            )
+            total[group] = product if first else total[group] + product
+
+    for step in range(1, half + 1):
+        for shot in range(shots):
+            for rightward in (True, False):
+                limit = reach(shot, rightward)
+                if step <= limit:
+                    arrival(step, shot, rightward).wait_recv()
+                if step + 1 <= limit:
+                    ring_copy(step + 1, shot, rightward).start()
+        if step == 1:
+            for block in range(chips):
+                own_copy(block).wait()
+                pair_copy(block).wait_recv()
+            multiply(chip, True)
+        multiply(chip_at(place - step))
+        if step < half:
+            multiply(chip_at(place + step))
+
+    lane = lax.broadcasted_iota(jnp.int32, (GROUP, 2 * width), 1)
+    diagonal = (lane % width) // (2 * rows) == lax.broadcasted_iota(
+        jnp.int32, (GROUP, 2 * width), 0
+    )
+    for group in range(groups):
+        for shot in range(shots):
+            for part in range(2):
+                start = (shot * 2 + part) * GROUP
+                piece = jnp.where(diagonal, total[group, start : start + GROUP, :], 0.0)
+                folded[part, shot : shot + 1, :] = jnp.sum(piece, axis=0, keepdims=True)
+        straight, crossed = folded[0], folded[1]
+        side = lax.broadcasted_iota(jnp.int32, (shots, 2 * width), 1) // rows % 2
+        ahead = pltpu.roll(crossed, 2 * width - rows, 1)
+        behind = pltpu.roll(crossed, rows, 1)
+        partials[group] = jnp.where(side == 0, straight - ahead, straight + behind)
+
+    share = freqs // n
+
+    def out_copy(step):
+        target = (me + step) % n
+        return pltpu.make_async_remote_copy(
+            src_ref=partials.at[target * share // GROUP],
+            dst_ref=landed.at[me],
+            send_sem=out_send.at[step - 1],
+            recv_sem=out_recv.at[step - 1],
+            device_id={"rows": target},
+            device_id_type=MESH,
+        )
+
+    def out_arrival(step):
+        source = (me + n - step) % n
+        return pltpu.make_async_remote_copy(
+            src_ref=partials.at[0],
+            dst_ref=landed.at[source],
+            send_sem=out_send.at[step - 1],
+            recv_sem=out_recv.at[step - 1],
+            device_id={"rows": source},
+            device_id_type=MESH,
+        )
+
+    for step in range(1, n):
+        out_copy(step).start()
+    landed[me] = partials[me * share // GROUP]
+    for step in range(1, n):
+        out_arrival(step).wait_recv()
+    for block in range(chips):
+        out_ref[block] = landed[2 * block] + landed[2 * block + 1]
+
+    for step in range(1, half + 1):
+        for shot in range(shots):
+            for rightward in (True, False):
+                if step <= reach(shot, rightward):
+                    ring_copy(step, shot, rightward).wait_send()
+    for block in range(chips):
+        pair_copy(block).wait_send()
+    for step in range(1, n):
+        out_copy(step).wait_send()
+
+
+def fused(n, traces, offset_bin, filters, data_matrix):
+    shots, receivers, length = traces.shape
+    freqs, _, rows, positions = data_matrix.shape
+    bin_count, taps = filters.shape
+    chips, half, groups, width = n // 2, n // 4, freqs // GROUP, GROUP * 2 * rows
+    head, lag, last = constants(freqs, length, taps, bin_count)
+    keep = np.arange(taps)[:, None] + np.arange(taps)[None, :] < taps
+    cut = jnp.where(keep[None], filters[:, None, :], 0.0).reshape(bin_count * taps, taps)
+    matrix = data_matrix.reshape(groups, width, positions)
+    dims = (n, shots, receivers, length, freqs, taps, bin_count, rows)
+    vmem = pl.BlockSpec(memory_space=pltpu.VMEM)
+    hbm = pl.BlockSpec(memory_space=pl.ANY)
+    dma = pltpu.SemaphoreType.DMA
+    landed = pl.pallas_call(
+        functools.partial(fused_kernel, dims),
+        out_shape=jax.ShapeDtypeStruct((chips, shots, 2 * width), jnp.float32),
+        in_specs=[hbm, vmem, vmem, vmem, vmem, vmem, vmem, hbm],
+        out_specs=vmem,
+        scratch_shapes=[
+            pltpu.VMEM((shots, receivers, length), jnp.bfloat16),
+            pltpu.VMEM((chips, shots, 2, freqs, receivers), jnp.bfloat16),
+            pltpu.VMEM((chips, groups, 2 * width, receivers), jnp.bfloat16),
+            pltpu.VMEM((groups, shots * 2 * GROUP, 2 * width), jnp.float32),
+            pltpu.VMEM((2 * freqs, bin_count * taps), jnp.bfloat16),
+            pltpu.VMEM((2, shots, 2 * width), jnp.float32),
+            pltpu.VMEM((groups, shots, 2 * width), jnp.float32),
+            pltpu.VMEM((n, shots, 2 * width), jnp.float32),
+            dma((shots,)), dma((chips,)), dma((chips,)), dma((chips,)),
+            dma((half, shots)), dma((half, shots)), dma((half, shots)), dma((half, shots)),
+            dma((n - 1,)), dma((n - 1,)),
+        ],
+        compiler_params=pltpu.CompilerParams(
+            collective_id=0, has_side_effects=True, vmem_limit_bytes=60 * 1024 * 1024
+        ),
+    )(traces, offset_bin, filters, cut, head, lag, last, matrix)
+    share = freqs // n
+    me = lax.axis_index("rows")
+    split = landed.reshape(chips, shots, 2, GROUP, 2, rows)
+    mine = lax.dynamic_slice_in_dim(split, me * share % GROUP, share, axis=3)
+    ordered = mine.transpose(3, 4, 1, 0, 2, 5)
+    return ordered.reshape(share, 2, shots, n * rows).astype(jnp.bfloat16)
+
+
+def shards(n, traces, offset_bin, filters, data_matrix):
+    freqs, _, rows, _ = data_matrix.shape
+    share = freqs // n
+    fits = (
+        n % 4 == 0 and traces.shape[1] % 128 == 0 and traces.shape[2] % 128 == 0
+        and freqs % GROUP == 0 and share > 0 and GROUP % share == 0
+        and GROUP * 2 * rows % 128 == 0 and filters.shape[1] <= 128
+    )
+    if fits:
+        return fused(n, traces, offset_bin, filters, data_matrix)
+    return plain(traces, offset_bin, filters, data_matrix)
+
+
 def solution(mesh):
     in_specs = (P("parts", "rows", None), P("parts", "rows"), P(), P("parts", None, "rows", None))
     out_specs = P(("parts", "rows"), None, None, None)
-    return jax.shard_map(shards, mesh=mesh, in_specs=in_specs, out_specs=out_specs, check_vma=False)
+    body = functools.partial(shards, mesh.shape["rows"])
+    return jax.shard_map(body, mesh=mesh, in_specs=in_specs, out_specs=out_specs, check_vma=False)

time: 368 us -> 66.3 us (0.18)
  other arithmetic: 225 us -> 1.42 us
  waiting for transfers between devices: 69.1 us -> 0 us
  Pallas kernels: 0 us -> 55.5 us
  local copies, waits for them, and re-layouts: 30 us -> 8.95 us
  matrix products: 20.2 us -> 0 us
  between operations: 13.6 us -> 0.05 us
  blocking collectives: 9.34 us -> 0 us
    convert_element_type x2 -> x0, other arithmetic: 223 us -> none  [the longest x1 223 us: condition(): return filtered.astype(jnp.bfloat16)]
    all_gather x1 -> x0, waiting for transfers between devices: 69.1 us -> none  [shards(): gathered = lax.all_gather(spectra, 'rows', axis=2, tiled=True)]
    pallas_call x0 -> x1, Pallas kernels: none -> 55.5 us  [fused(): pl.pallas_call(functools.partial(fused_kernel, dims), out_shape=jax.Shape...]
    dot_general x6 -> x0, matrix products: 20.2 us -> none  [the longest x1 6.26 us: spectra_of(): lax.dot_general(flat_table, flat_signal, (((1,), (1,)), ((), ())), prefer...]
    reshape x3 -> x1, local copies, waits for them, and re-layouts: 23.1 us -> 6.92 us  [fused(): matrix = data_matrix.reshape(groups, width, positions)]
    all_to_all x1 -> x0, blocking collectives: 9.34 us -> none  [shards(): lax.all_to_all(partial_value.astype(jnp.bfloat16), 'rows', split_axis=0,...]
    slice x3 -> x0, local copies, waits for them, and re-layouts: 4.26 us -> none  [the longest x1 4.07 us: predict(): matrix_block[:, 1]]
  transfers between devices with their start and end apart: 1 -> 0, of which waited for: 1 -> 0; matrix products, arithmetic and copies ran while one was open for 3% -> 0% of each run, Pallas kernels for 0% -> 0%
where the time goes in v1:
time: 66.3 us; the launch traced here: 65.9 us
  Pallas kernels  55.5 us (84%)
  local copies, waits for them, and re-layouts  8.95 us (13%)
  other arithmetic  1.42 us (2%)
    pallas_call x1, Pallas kernels, fused(): pl.pallas_call(functools.partial(fused_kernel, dims), out_shape=jax.Shape...  55.5 us
    reshape x1, local copies, waits for them, and re-layouts, fused(): matrix = data_matrix.reshape(groups, width, positions)  6.92 us
    select_n x1, other arithmetic, fused(): jnp.where(keep[None], filters[:, None, :], 0.0)  1.42 us

profile of v1, /device:TPU:0, one launch (start us, length us, event | category | flops | bytes accessed | tf_op | source)
XLA Modules:
  0.0 65.9 jit_solution(17687554253201555755)
XLA Ops:
  0.0 1.4 %broadcast_select_fusion = f32[16,32,32]{2,1,0:T(8,128)} fusion(f32[16,32]{1,0:T(8,128)} %filters_ref.1, pred[32,32]{1,0:T(8,128)(4,1)} %bitcast.9), kind=kLoop, calls=%fused_computation.2 | loop fusion | flops 16384 | bytes 68608 | tf_op jit(solution)/shard_map/jit(_where)/select_n | solution.py:338
  1.4 6.9 %reshape.14.matrix_hbm = bf16[4,128,4096]{2,1,0:T(8,128)(2,1)} reshape(bf16[64,2,4,4096]{3,2,1,0:T(4,128)(2,1)} %param.11) | data formatting | bytes 8388608 | tf_op jit(solution)/shard_map/reshape | solution.py:339
  8.3 55.5 %shard_map.82 = f32[8,8,256]{2,1,0:T(8,128)} custom-call(bf16[8,256,2048]{2,1,0:T(8,128)(2,1)} %traces_hbm.1, s32[8,256]{1,0:T(8,128)} %bins_ref.1, f32[16,32]{1,0:T(8,128)} %filters_ref.1, f32[512,32]{1,0:T(8,128)} %bitcast.6, bf16[128,2048]{1,0:T(8,128)(2,1)} %constant.31.clone.head_ref, f32[128,32]{1,0:T(8,128)} %constant.32.clone.lag_ref, ...), custom_call_target="tpu_custom_call" | custom-call | tf_op jit(solution)/shard_map/pallas_call | solution.py:344
  63.8 1.3 %copy.10 = bf16[8,8,256]{1,0,2:T(8,128)(2,1)S(1)} copy(f32[8,8,256]{2,1,0:T(8,128)} %shard_map.82) | data formatting | bytes 98304 | tf_op jit(solution)/shard_map/pallas_call | solution.py:344
  65.1 0.1 copy.11
  65.2 0.7 %copy.12 = bf16[4,2,8,64]{3,2,1,0:T(8,128)(2,1)} copy(bf16[4,2,8,64]{2,3,1,0:T(8,128)(2,1)S(1)} %bitcast.8) | data formatting | bytes 16384 | tf_op jit(solution)/shard_map/convert_element_type | solution.py:371
  (1 shorter events, 0.0 us)

commit v2 on v1

--- a/solution.py
+++ b/solution.py
@@ -114,7 +114,7 @@
 
 
 def fused_kernel(
-    dims, traces_hbm, bins_ref, filters_ref, cut_ref, head_ref, lag_ref, last_ref, matrix_hbm,
+    dims, traces_hbm, bins_ref, filters_ref, head_ref, lag_ref, last_ref, matrix_hbm,
     out_ref,
     traces_buf, spectra, matrix_buf, total, tail_ref, folded, partials, landed,
     trace_sem, own_sem, pair_send, pair_recv,
@@ -151,20 +151,17 @@
     def columns(block, side):
         return pl.ds(pl.multiple_of((block * 2 + side) * receivers, receivers), receivers)
 
-    def lanes():
-        return pl.ds(pl.multiple_of(core * width, width), width)
-
     def own_copy(block):
         return pltpu.make_async_copy(
-            matrix_hbm.at[:, :, columns(block, core)],
-            matrix_buf.at[block, :, lanes(), :],
+            matrix_hbm.at[:, :, :, columns(block, core)],
+            matrix_buf.at[block, core],
             own_sem.at[block],
         )
 
     def pair_copy(block):
         return pltpu.make_async_remote_copy(
-            src_ref=matrix_hbm.at[:, :, columns(block, 1 - core)],
-            dst_ref=matrix_buf.at[block, :, lanes(), :],
+            src_ref=matrix_hbm.at[:, :, :, columns(block, 1 - core)],
+            dst_ref=matrix_buf.at[block, core],
             send_sem=pair_send.at[block],
             recv_sem=pair_recv.at[block],
             device_id={"rows": sibling},
@@ -204,8 +201,13 @@
         lag_ref[...], filters_ref[...], contract, precision=highest,
         preferred_element_type=jnp.float32,
     )
+    taps_cube = (bin_count, taps, taps)
+    delay = sum(lax.broadcasted_iota(jnp.int32, taps_cube, axis) for axis in (1, 2))
+    kept = jnp.where(
+        delay < taps, jnp.broadcast_to(filters_ref[...][:, None, :], taps_cube), 0.0
+    )
     cut = lax.dot_general(
-        lag_ref[...], cut_ref[...], contract, precision=highest,
+        lag_ref[...], kept.reshape(bin_count * taps, taps), contract, precision=highest,
         preferred_element_type=jnp.float32,
     )
     cut_re, cut_im = cut[:freqs], cut[freqs:]
@@ -246,8 +248,11 @@
     def multiply(block, first=False):
         for group in range(groups):
             signal = spectra[block, :, :, group * GROUP : (group + 1) * GROUP, :]
+            matrix = matrix_buf[block, :, group * GROUP : (group + 1) * GROUP]
             product = lax.dot_general(
-                signal.reshape(shots * 2 * GROUP, receivers), matrix_buf[block, group], contract,
+                signal.reshape(shots * 2 * GROUP, receivers),
+                matrix.reshape(2 * width, receivers),
+                contract,
                 preferred_element_type=jnp.float32,
             )
             total[group] = product if first else total[group] + product
@@ -334,9 +339,6 @@
     bin_count, taps = filters.shape
     chips, half, groups, width = n // 2, n // 4, freqs // GROUP, GROUP * 2 * rows
     head, lag, last = constants(freqs, length, taps, bin_count)
-    keep = np.arange(taps)[:, None] + np.arange(taps)[None, :] < taps
-    cut = jnp.where(keep[None], filters[:, None, :], 0.0).reshape(bin_count * taps, taps)
-    matrix = data_matrix.reshape(groups, width, positions)
     dims = (n, shots, receivers, length, freqs, taps, bin_count, rows)
     vmem = pl.BlockSpec(memory_space=pltpu.VMEM)
     hbm = pl.BlockSpec(memory_space=pl.ANY)
@@ -344,12 +346,12 @@
     landed = pl.pallas_call(
         functools.partial(fused_kernel, dims),
         out_shape=jax.ShapeDtypeStruct((chips, shots, 2 * width), jnp.float32),
-        in_specs=[hbm, vmem, vmem, vmem, vmem, vmem, vmem, hbm],
+        in_specs=[hbm, vmem, vmem, vmem, vmem, vmem, hbm],
         out_specs=vmem,
         scratch_shapes=[
             pltpu.VMEM((shots, receivers, length), jnp.bfloat16),
             pltpu.VMEM((chips, shots, 2, freqs, receivers), jnp.bfloat16),
-            pltpu.VMEM((chips, groups, 2 * width, receivers), jnp.bfloat16),
+            pltpu.VMEM((chips, 2, freqs, 2, rows, receivers), jnp.bfloat16),
             pltpu.VMEM((groups, shots * 2 * GROUP, 2 * width), jnp.float32),
             pltpu.VMEM((2 * freqs, bin_count * taps), jnp.bfloat16),
             pltpu.VMEM((2, shots, 2 * width), jnp.float32),
@@ -362,7 +364,7 @@
         compiler_params=pltpu.CompilerParams(
             collective_id=0, has_side_effects=True, vmem_limit_bytes=60 * 1024 * 1024
         ),
-    )(traces, offset_bin, filters, cut, head, lag, last, matrix)
+    )(traces, offset_bin, filters, head, lag, last, data_matrix)
     share = freqs // n
     me = lax.axis_index("rows")
     split = landed.reshape(chips, shots, 2, GROUP, 2, rows)

time: 66.3 us -> 57.6 us (0.87)
  local copies, waits for them, and re-layouts: 8.95 us -> 2.04 us
  other arithmetic: 1.42 us -> 0 us
    reshape x1 -> x0, local copies, waits for them, and re-layouts: 6.92 us -> none  [fused(): matrix = data_matrix.reshape(groups, width, positions)]
    select_n x1 -> x0, other arithmetic: 1.42 us -> none  [fused(): jnp.where(keep[None], filters[:, None, :], 0.0)]
where the time goes in v2:
time: 57.6 us; the launch traced here: 57.4 us
  Pallas kernels  55.4 us (96%)
  local copies, waits for them, and re-layouts  2.04 us (4%)
    pallas_call x1, Pallas kernels, fused(): pl.pallas_call(functools.partial(fused_kernel, dims), out_shape=jax.Shape...  55.4 us
    pallas_call x1, local copies, waits for them, and re-layouts, fused(): pl.pallas_call(functools.partial(fused_kernel, dims), out_shape=jax.Shape...  1.26 us

profile of v2, /device:TPU:0, one launch (start us, length us, event | category | flops | bytes accessed | tf_op | source)
XLA Modules:
  0.0 57.4 jit_solution(9331963039284296054)
XLA Ops:
  0.0 55.4 %shard_map.73 = f32[8,8,256]{2,1,0:T(8,128)} custom-call(bf16[8,256,2048]{2,1,0:T(8,128)(2,1)} %traces_hbm.1, s32[8,256]{1,0:T(8,128)} %bins_ref.1, f32[16,32]{1,0:T(8,128)} %filters_ref.1, bf16[128,2048]{1,0:T(8,128)(2,1)} %constant.26.clone.head_ref, f32[128,32]{1,0:T(8,128)} %constant.27.clone.lag_ref, f32[2,64,512]{2,1,0:T(8,128)} %constant.28.clone.last_ref, ...), custom_call_target="tpu_custom_call" | custom-call | tf_op jit(solution)/shard_map/pallas_call | solution.py:346
  55.4 1.3 %copy.9 = bf16[8,8,256]{1,0,2:T(8,128)(2,1)S(1)} copy(f32[8,8,256]{2,1,0:T(8,128)} %shard_map.73) | data formatting | bytes 98304 | tf_op jit(solution)/shard_map/pallas_call | solution.py:346
  56.7 0.1 copy.10
  56.7 0.7 %copy.11 = bf16[4,2,8,64]{3,2,1,0:T(8,128)(2,1)} copy(bf16[4,2,8,64]{2,3,1,0:T(8,128)(2,1)S(1)} %bitcast.5) | data formatting | bytes 16384 | tf_op jit(solution)/shard_map/convert_element_type | solution.py:373
  (1 shorter events, 0.0 us)

commit v3 on v2

--- a/solution.py
+++ b/solution.py
@@ -278,6 +278,8 @@
     diagonal = (lane % width) // (2 * rows) == lax.broadcasted_iota(
         jnp.int32, (GROUP, 2 * width), 0
     )
+    share = freqs // n
+    span = 2 * rows * share
     for group in range(groups):
         for shot in range(shots):
             for part in range(2):
@@ -288,14 +290,19 @@
         side = lax.broadcasted_iota(jnp.int32, (shots, 2 * width), 1) // rows % 2
         ahead = pltpu.roll(crossed, 2 * width - rows, 1)
         behind = pltpu.roll(crossed, rows, 1)
-        partials[group] = jnp.where(side == 0, straight - ahead, straight + behind)
-
-    share = freqs // n
+        result = jnp.where(side == 0, straight - ahead, straight + behind)
+        for window in range(GROUP // share):
+            start = 2 * width - window * span
+            partials[group * (GROUP // share) + window] = jnp.where(
+                lax.broadcasted_iota(jnp.int32, (shots, width), 1) < span,
+                pltpu.roll(result[:, :width], start % width, 1),
+                pltpu.roll(result[:, width:], (start + span) % width, 1),
+            )
 
     def out_copy(step):
         target = (me + step) % n
         return pltpu.make_async_remote_copy(
-            src_ref=partials.at[target * share // GROUP],
+            src_ref=partials.at[target],
             dst_ref=landed.at[me],
             send_sem=out_send.at[step - 1],
             recv_sem=out_recv.at[step - 1],
@@ -314,13 +321,15 @@
             device_id_type=MESH,
         )
 
-    for step in range(1, n):
+    for step in sorted(range(1, n), key=lambda step: abs(step - n // 2)):
         out_copy(step).start()
-    landed[me] = partials[me * share // GROUP]
+    landed[me] = partials[me]
     for step in range(1, n):
         out_arrival(step).wait_recv()
     for block in range(chips):
-        out_ref[block] = landed[2 * block] + landed[2 * block + 1]
+        summed = landed[2 * block] + landed[2 * block + 1]
+        out_ref[:, 2 * block, :] = summed[:, :span]
+        out_ref[:, 2 * block + 1, :] = summed[:, span : 2 * span]
 
     for step in range(1, half + 1):
         for shot in range(shots):
@@ -335,7 +344,8 @@
 
 def fused(n, traces, offset_bin, filters, data_matrix):
     shots, receivers, length = traces.shape
-    freqs, _, rows, positions = data_matrix.shape
+    freqs, _, rows, _ = data_matrix.shape
+    share = freqs // n
     bin_count, taps = filters.shape
     chips, half, groups, width = n // 2, n // 4, freqs // GROUP, GROUP * 2 * rows
     head, lag, last = constants(freqs, length, taps, bin_count)
@@ -345,7 +355,7 @@
     dma = pltpu.SemaphoreType.DMA
     landed = pl.pallas_call(
         functools.partial(fused_kernel, dims),
-        out_shape=jax.ShapeDtypeStruct((chips, shots, 2 * width), jnp.float32),
+        out_shape=jax.ShapeDtypeStruct((shots, n, 2 * rows * share), jnp.float32),
         in_specs=[hbm, vmem, vmem, vmem, vmem, vmem, hbm],
         out_specs=vmem,
         scratch_shapes=[
@@ -355,8 +365,8 @@
             pltpu.VMEM((groups, shots * 2 * GROUP, 2 * width), jnp.float32),
             pltpu.VMEM((2 * freqs, bin_count * taps), jnp.bfloat16),
             pltpu.VMEM((2, shots, 2 * width), jnp.float32),
-            pltpu.VMEM((groups, shots, 2 * width), jnp.float32),
-            pltpu.VMEM((n, shots, 2 * width), jnp.float32),
+            pltpu.VMEM((n, shots, width), jnp.float32),
+            pltpu.VMEM((n, shots, width), jnp.float32),
             dma((shots,)), dma((chips,)), dma((chips,)), dma((chips,)),
             dma((half, shots)), dma((half, shots)), dma((half, shots)), dma((half, shots)),
             dma((n - 1,)), dma((n - 1,)),
@@ -365,12 +375,8 @@
             collective_id=0, has_side_effects=True, vmem_limit_bytes=60 * 1024 * 1024
         ),
     )(traces, offset_bin, filters, head, lag, last, data_matrix)
-    share = freqs // n
-    me = lax.axis_index("rows")
-    split = landed.reshape(chips, shots, 2, GROUP, 2, rows)
-    mine = lax.dynamic_slice_in_dim(split, me * share % GROUP, share, axis=3)
-    ordered = mine.transpose(3, 4, 1, 0, 2, 5)
-    return ordered.reshape(share, 2, shots, n * rows).astype(jnp.bfloat16)
+    ordered = landed.astype(jnp.bfloat16).reshape(shots, n, share, 2, rows)
+    return ordered.transpose(2, 3, 0, 1, 4).reshape(share, 2, shots, n * rows)
 
 
 def shards(n, traces, offset_bin, filters, data_matrix):
@@ -378,7 +384,7 @@
     share = freqs // n
     fits = (
         n % 4 == 0 and traces.shape[1] % 128 == 0 and traces.shape[2] % 128 == 0
-        and freqs % GROUP == 0 and share > 0 and GROUP % share == 0
+        and freqs % GROUP == 0 and share > 0 and GROUP % (2 * share) == 0
         and GROUP * 2 * rows % 128 == 0 and filters.shape[1] <= 128
     )
     if fits:

time: 57.6 us -> 57.2 us (level)
  local copies, waits for them, and re-layouts: 2.04 us -> 0.95 us
  other arithmetic: 0 us -> 0.85 us
    pallas_call x1 -> x0, local copies, waits for them, and re-layouts: 1.26 us -> none  [fused(): pl.pallas_call(functools.partial(fused_kernel, dims), out_shape=jax.Shape...]
    convert_element_type x0 -> x1, other arithmetic: none -> 0.85 us  [fused(): ordered = landed.astype(jnp.bfloat16).reshape(shots, n, share, 2, rows)]
    reshape x0 -> x1, local copies, waits for them, and re-layouts: none -> 0.71 us  [fused(): return ordered.transpose(2, 3, 0, 1, 4).reshape(share, 2, shots, n * rows)]
    convert_element_type x3 -> x1, local copies, waits for them, and re-layouts: 0.78 us -> 0.11 us  [fused(): ordered = landed.astype(jnp.bfloat16).reshape(shots, n, share, 2, rows)]
where the time goes in v3:
time: 57.2 us; the launch traced here: 57 us
  Pallas kernels  55.2 us (97%)
  local copies, waits for them, and re-layouts  0.95 us (2%)
  other arithmetic  0.85 us (1%)
    pallas_call x1, Pallas kernels, fused(): pl.pallas_call(functools.partial(fused_kernel, dims), out_shape=jax.Shape...  55.2 us

profile of v3, /device:TPU:0, one launch (start us, length us, event | category | flops | bytes accessed | tf_op | source)
XLA Modules:
  0.0 57.0 jit_solution(18271639986478553791)
XLA Ops:
  0.0 55.2 %shard_map.73 = f32[8,16,32]{2,1,0:T(8,128)} custom-call(bf16[8,256,2048]{2,1,0:T(8,128)(2,1)} %traces_hbm.1, s32[8,256]{1,0:T(8,128)} %bins_ref.1, f32[16,32]{1,0:T(8,128)} %filters_ref.1, bf16[128,2048]{1,0:T(8,128)(2,1)} %constant.6.clone.head_ref, f32[128,32]{1,0:T(8,128)} %constant.7.clone.lag_ref, f32[2,64,512]{2,1,0:T(8,128)} %constant.8.clone.last_ref, ...), custom_call_target="tpu_custom_call" | custom-call | tf_op jit(solution)/shard_map/pallas_call | solution.py:356
  55.2 0.8 %convert_element_type.3 = bf16[8,16,32]{2,1,0:T(8,128)(2,1)S(1)} convert(f32[8,16,32]{2,1,0:T(8,128)} %shard_map.73) | non-fusion elementwise | flops 4096 | bytes 24576 | tf_op jit(solution)/shard_map/convert_element_type | solution.py:378
  56.1 0.1 copy.9
  56.2 0.1 copy.10
  56.3 0.7 %copy.11 = bf16[4,2,8,64]{3,2,1,0:T(8,128)(2,1)} copy(bf16[4,2,8,64]{2,3,1,0:T(8,128)(2,1)S(1)} %bitcast.4) | data formatting | bytes 16384 | tf_op jit(solution)/shard_map/reshape | solution.py:379
